TPU v7x, 256 devices: a whole 4x4x8 slice. The times are simulated.
256 devices in a mesh: loop: 64 (over x, y_hi, z), grp: 4 (over y_lo, core).
Axes of the slice: x: 4, y: 4 (y_hi: 2, y_lo: 2; y = y_hi * 2 + y_lo), z: 8, core: 2. Of those that a mesh axis runs over, the one named last changes fastest.
Arguments:
- student_image: bfloat16 [98304, 768], P(('loop', 'grp')), may hold values from -64 to 64
- student_text: bfloat16 [98304, 768], P(('loop', 'grp')), may hold values from -64 to 64
- teacher_image: bfloat16 [98304, 1152], P(('loop', 'grp')), may hold values from -64 to 64
- teacher_text: bfloat16 [98304, 1152], P(('loop', 'grp')), may hold values from -64 to 64
- student_scale: float32 [1], replicated, may hold values from 10 to 40
- student_bias: float32 [1], replicated, may hold values from -3 to 1
- teacher_scale: float32 [1], replicated, may hold values from 50 to 150
- teacher_bias: float32 [1], replicated, may hold values from -4 to 0
Outputs:
- grad_image: float32 [98304, 768], P(('loop', 'grp'))
- grad_text: float32 [98304, 768], P(('loop', 'grp'))
All inputs are finite; a program needn't handle non-finite values.
Results may differ from a plain program's by a relative error of at most 0.0065.
Values may be sent and summed in bfloat16 or wider, within the bound.
A program may use at most 64 MiB of HBM per device.

v0:
```python
import jax
import jax.numpy as jnp
from jax import lax
from jax.sharding import PartitionSpec as P

STEPS = 2


def shifted(block, axis, distance):
    devices = range(lax.axis_size(axis))
    route = [((i - distance) % len(devices), i) for i in devices]
    return lax.ppermute(block, axis, route)


def unit_rows(values):
    wide = values.astype(jnp.float32)
    inverse = lax.rsqrt(jnp.sum(wide * wide, axis=-1, keepdims=True) + 1e-06)
    return (wide * inverse, inverse)


def tile_terms(image_half, teach_image, text_block, teach_block, scales):
    student_scale, student_bias, teacher_scale, teacher_bias = scales
    teach = jnp.einsum("id,jd->ij", teach_image, teach_block, preferred_element_type=jnp.float32)
    target = jax.nn.sigmoid(teacher_scale * teach + teacher_bias)
    logits = (
        student_scale
        * jnp.einsum("id,jd->ij", image_half, text_block, preferred_element_type=jnp.float32)
        + student_bias
    )
    weight = (jax.nn.sigmoid(logits) - target).astype(jnp.bfloat16)
    image_pull = jnp.dot(weight, text_block, preferred_element_type=jnp.float32)
    text_pull = jnp.einsum("ij,id->jd", weight, image_half, preferred_element_type=jnp.float32)
    return (image_pull, text_pull)


def project_out(pull, unit, inverse, scale):
    grown = scale * pull
    return (grown - unit * jnp.sum(unit * grown, axis=-1, keepdims=True)) * inverse


def per_device(
    student_image,
    student_text,
    teacher_image,
    teacher_text,
    student_scale,
    student_bias,
    teacher_scale,
    teacher_bias,
):
    scales = (student_scale, student_bias, teacher_scale, teacher_bias)
    image_unit, image_inv = unit_rows(student_image)
    text_unit, text_inv = unit_rows(student_text)
    image_half = image_unit.astype(jnp.bfloat16)
    text_half = text_unit.astype(jnp.bfloat16)
    teach_image = unit_rows(teacher_image)[0].astype(jnp.bfloat16)
    teach_text = unit_rows(teacher_text)[0].astype(jnp.bfloat16)
    image_total = jnp.zeros(image_half.shape, jnp.float32)
    pulls = []
    text_block, teach_block = (
        lax.all_gather(text_half, "grp", axis=0, tiled=True),
        lax.all_gather(teach_text, "grp", axis=0, tiled=True),
    )
    for offset in range(STEPS):
        if offset > 0:
            text_block, teach_block = shifted((text_block, teach_block), "loop", 1)
        image_pull, text_pull = tile_terms(image_half, teach_image, text_block, teach_block, scales)
        image_total = image_total + image_pull
        pulls.append(text_pull)
    carried = pulls[-1]
    offset = 0
    carried = shifted(carried, "loop", -1) + pulls[offset]
    text_total = lax.psum_scatter(carried, "grp", scatter_dimension=0, tiled=True)
    grad_image = project_out(image_total, image_unit, image_inv, student_scale)
    grad_text = project_out(text_total, text_unit, text_inv, student_scale)
    return (grad_image, grad_text)


def solution(mesh):
    return jax.shard_map(
        per_device,
        mesh=mesh,
        in_specs=(
            P(("loop", "grp"), None),
            P(("loop", "grp"), None),
            P(("loop", "grp"), None),
            P(("loop", "grp"), None),
            P(),
            P(),
            P(),
            P(),
        ),
        out_specs=(P(("loop", "grp"), None), P(("loop", "grp"), None)),
        check_vma=False,
    )
```

profile of v0, /device:TPU:1, one launch (start us, length us, event | category | flops | bytes accessed | tf_op | source)
XLA Modules:
  0.0 388.5 jit_solution(17114492417577123373)
XLA Ops:
  7.2 0.0 copy-start.1
  7.2 0.0 all-gather.5.cloned.1.call-start
  7.2 1.5 fusion.26
  8.7 2.3 fusion.27
  11.0 0.0 copy-start
  11.0 0.0 all-gather.5.cloned.1.call-update
  11.0 0.0 all-gather.3.cloned.1.call-start
  11.1 0.0 copy-done.1
  11.1 0.2 fusion.42
  11.3 1.0 fusion.30
  12.3 0.0 all-gather.3.cloned.1.call-update
  12.3 0.0 reduce-scatter.2.cloned.1.call-start
  12.3 46.7 %all-gather.5.cloned.1.call-done = bf16[1536,1152]{1,0:T(8,128)(2,1)} async-done(((bf16[384,1152]{1,0:T(8,128)(2,1)}), bf16[1536,1152]{1,0:T(8,128)(2,1)}) %all-gather.5.cloned.1.call-update) | async-done | bytes 3538960 | tf_op jit(solution)/shard_map/all_gather | solution.py:62
  59.1 1.3 collective-permute-start.1
  60.3 99.8 %all-gather.3.cloned.1.call-done = bf16[1536,768]{1,0:T(8,128)(2,1)} async-done(((bf16[384,768]{1,0:T(8,128)(2,1)}), bf16[1536,768]{1,0:T(8,128)(2,1)}) %all-gather.3.cloned.1.call-update) | async-done | bytes 2359312 | tf_op jit(solution)/shard_map/all_gather | solution.py:61
  160.1 0.0 collective-permute-start
  162.7 0.0 copy-done
  162.7 0.2 fusion.38
  162.9 0.0 copy-done.3
  162.9 0.3 fusion.24
  163.2 0.0 collective-permute-done.1
  163.2 4.0 %fusion.16 = f32[384,1536]{1,0:T(8,128)S(1)} fusion(bf16[1536,1152]{1,0:T(8,128)(2,1)} %collective-permute-done.1, f32[]{:T(128)} %bitcast.24, f32[]{:T(128)} %bitcast.22, bf16[384,1152]{1,0:T(8,128)(2,1)S(1)} %copy-done.3, f32[384]{0:T(512)S(1)} %add_rsqrt_fusion.1), kind=kOutput, calls=%fused_computation.21 | convolution fusion | flops 1363230720 | bytes 6784520 | tf_op jit(solution)/shard_map/id,jd->ij/dot_general | solution.py:23
  167.1 51.3 %collective-permute-done = bf16[1536,768]{1,0:T(8,128)(2,1)S(1)} collective-permute-done((bf16[1536,768]{1,0:T(8,128)(2,1)}, bf16[1536,768]{1,0:T(8,128)(2,1)S(1)}, u32[]{:S(2)}, u32[]{:S(2)}) %collective-permute-start) | collective-permute-done | bytes 2359328 | tf_op jit(solution)/shard_map/ppermute | solution.py:12
  218.4 0.0 copy-start.7
  218.4 1.4 fusion.23
  219.8 0.0 copy-done.7
  219.9 0.0 copy-start.6
  219.9 1.5 fusion.46
  221.4 0.3 collective-permute-start.2
  221.6 0.0 copy-done.6
  221.6 0.0 copy-start.4
  221.6 0.0 copy-start.5
  221.7 1.4 fusion.20
  223.0 0.0 copy-done.4
  223.0 0.9 copy-done.5
  223.9 2.0 fusion.19
  225.9 97.7 %collective-permute-done.2 = f32[1536,768]{1,0:T(8,128)S(1)} collective-permute-done((f32[1536,768]{1,0:T(8,128)S(1)}, f32[1536,768]{1,0:T(8,128)S(1)}, u32[]{:S(2)}, u32[]{:S(2)}) %collective-permute-start.2) | collective-permute-done | bytes 4718624 | tf_op jit(solution)/shard_map/ppermute | solution.py:12
  323.7 3.6 convolution_add_fusion
  327.3 0.0 reduce-scatter.2.cloned.1.call-update
  327.3 0.0 copy-start.8
  327.3 2.9 fusion.50
  330.2 0.0 copy-done.8
  330.2 1.2 fusion.35
  331.4 1.3 fusion.37
  332.7 46.3 %reduce-scatter.2.cloned.1.call-done = f32[384,768]{1,0:T(8,128)} async-done(((f32[1536,768]{1,0:T(8,128)}), f32[384,768]{1,0:T(8,128)}) %reduce-scatter.2.cloned.1.call-update) | async-done | bytes 1179664 | tf_op jit(solution)/shard_map/reduce_scatter | solution.py:73
  379.0 1.7 fusion.39
  380.7 0.0 copy-done.2
  380.7 1.3 fusion.41
  (6 shorter events, 0.0 us)
Async XLA Ops:
  7.2 3.9 %copy-start.1 = (bf16[384,768]{1,0:T(8,128)(2,1)S(1)}, bf16[384,768]{1,0:T(8,128)(2,1)}, u32[]{:S(2)}) copy-start(bf16[384,768]{1,0:T(8,128)(2,1)} %param.9) | copy-start | bytes 1769476
  7.2 51.9 %all-gather.5.cloned.1.call-start = ((), (), s32[]{:S(2)}) async-start(), calls=%async_computation.2 | async-start | bytes 4423680 | tf_op jit(solution)/shard_map/all_gather | solution.py:62
  11.0 151.7 %copy-start = (bf16[384,768]{1,0:T(8,128)(2,1)S(1)}, bf16[384,768]{1,0:T(8,128)(2,1)}, u32[]{:S(2)}) copy-start(bf16[384,768]{1,0:T(8,128)(2,1)} %param.8) | copy-start | bytes 1769476
  11.0 151.9 %copy-start.3 = (bf16[384,1152]{1,0:T(8,128)(2,1)S(1)}, bf16[384,1152]{1,0:T(8,128)(2,1)}, u32[]{:S(2)}) copy-start(bf16[384,1152]{1,0:T(8,128)(2,1)} %param.10) | copy-start | bytes 2654212
  11.0 149.1 %all-gather.3.cloned.1.call-start = ((), (), s32[]{:S(2)}) async-start(), calls=%async_computation.1 | async-start | bytes 2949120 | tf_op jit(solution)/shard_map/all_gather | solution.py:61
  12.3 366.7 %reduce-scatter.2.cloned.1.call-start = ((), (), s32[]{:S(2)}) async-start(), calls=%async_computation.3 | async-start | bytes 5898240 | tf_op jit(solution)/shard_map/reduce_scatter | solution.py:73
  59.1 104.1 %collective-permute-start.1 = (bf16[1536,1152]{1,0:T(8,128)(2,1)}, bf16[1536,1152]{1,0:T(8,128)(2,1)}, u32[]{:S(2)}, u32[]{:S(2)}) collective-permute-start(bf16[1536,1152]{1,0:T(8,128)(2,1)} %all-gather.5.cloned.1.call-done), channel_id=1, source_target_pairs={{252,0},{0,4},{4,8},{8,12},{12,16},{16,20},{20,24},{24,28},{28,32}... | collective-permute-start | bytes 10616840 | tf_op jit(solution)/shard_map/ppermute | solution.py:12
  160.1 58.3 %collective-permute-start = (bf16[1536,768]{1,0:T(8,128)(2,1)}, bf16[1536,768]{1,0:T(8,128)(2,1)S(1)}, u32[]{:S(2)}, u32[]{:S(2)}) collective-permute-start(bf16[1536,768]{1,0:T(8,128)(2,1)} %all-gather.3.cloned.1.call-done), channel_id=1, source_target_pairs={{252,0},{0,4},{4,8},{8,12},{12,16},{16,20},{20,24},{24,28},{28,32}... | collective-permute-start | bytes 7077896 | tf_op jit(solution)/shard_map/ppermute | solution.py:12
  218.4 1.4 copy-start.7
  219.9 1.8 copy-start.6
  221.4 102.3 %collective-permute-start.2 = (f32[1536,768]{1,0:T(8,128)S(1)}, f32[1536,768]{1,0:T(8,128)S(1)}, u32[]{:S(2)}, u32[]{:S(2)}) collective-permute-start(f32[1536,768]{1,0:T(8,128)S(1)} %fusion.46), channel_id=1, source_target_pairs={{4,0},{8,4},{12,8},{16,12},{20,16},{24,20},{28,24},{32,28},{36,32}... | collective-permute-start | bytes 14155784 | tf_op jit(solution)/shard_map/ppermute | solution.py:12
  221.6 1.4 copy-start.4
  221.6 2.3 copy-start.5
  327.3 2.9 copy-start.8
  379.0 1.7 copy-start.2
Sparse Core Ops, SparseCore 0:
  11.1 47.8 all-gather.4
  61.4 98.6 all-gather.2
  327.4 51.5 reduce-scatter.1
where the time goes:
time: 389 us
  waiting for transfers between devices  342 us (88%)
  matrix products  18 us (5%)
  between operations  16.5 us (4%)
  other arithmetic  9.71 us (2%)
    ppermute x3, waiting for transfers between devices, shifted(): return lax.ppermute(block, axis, route)  149 us
    all_gather x1, waiting for transfers between devices, per_device(): lax.all_gather(text_half, 'grp', axis=0, tiled=True)  99.8 us
    all_gather x1, waiting for transfers between devices, per_device(): lax.all_gather(teach_text, 'grp', axis=0, tiled=True)  46.7 us
    reduce_scatter x1, waiting for transfers between devices, per_device(): lax.psum_scatter(carried, 'grp', scatter_dimension=0, tiled=True)  46.3 us
  transfers between devices with their start and end apart: 6, of which 5 were waited for; matrix products, arithmetic and copies ran while one was open for 4% of the time, Pallas kernels for 0%

commit v1 on v0

v1 whole, which is shorter than its diff:
```python
import functools

import jax
import jax.numpy as jnp
from jax import lax
from jax.experimental import pallas as pl
from jax.experimental.pallas import tpu as pltpu
from jax.sharding import PartitionSpec as P

MESH = pl.DeviceIdType.MESH
N_LOOP = 64
RUN = 8
ROWS = 384
D_S = 768
D_T = 1152
CHUNKS = ((0, 128), (128, 128), (256, 64), (320, 64))
N_CH = len(CHUNKS)
PULL = 64
N_PULL = ROWS // PULL
OWN_TEXT = 2 * ROWS

NT = (((1,), (1,)), ((), ()))
TN = (((0,), (0,)), ((), ()))


def partners():
    loop = lax.axis_index("loop")
    grp = lax.axis_index("grp")
    chip = grp // 2
    core = grp % 2
    seam_next = ((loop % RUN) + 1) // RUN
    seam_prev = (((N_LOOP - loop) % RUN) + RUN - 1) // RUN
    seam_prev = 1 - seam_prev
    across = (loop, (1 - chip) * 2 + core)
    sibling = (loop, chip * 2 + 1 - core)
    after = ((loop + 1) % N_LOOP, ((chip + seam_next) % 2) * 2 + core)
    before = ((loop + N_LOOP - 1) % N_LOOP, ((chip + seam_prev) % 2) * 2 + core)
    return across, sibling, after, before


def kernel(
    ss_ref, sb_ref, ts_ref, tb_ref, si_hbm, st_hbm, ti_hbm, tt_hbm, gi_hbm, gt_hbm,
    raw_si, raw_st, raw_ti, raw_tt, inv_i, inv_t,
    SI, TI, ST, TT, TG, W,
    img_own, txt_own, prev_own,
    y_out, y_in, dt_out, dt_in, dp_out, dp_in, z_out, z_in,
    gi_buf, gt_buf,
    in_sem, out_sem,
    y_s, y_r, z_s, z_r, d_s, d_r, f_s, f_r,
    yp_s, yp_r, dt_s, dt_r, dp_s, dp_r, zp_s, zp_r,
):
    across, sibling, after, before = partners()
    s_scale, s_bias, t_scale, t_bias = ss_ref[0], sb_ref[0], ts_ref[0], tb_ref[0]

    def remote(src, dst, ssem, rsem, dev):
        return pltpu.make_async_remote_copy(
            src_ref=src, dst_ref=dst, send_sem=ssem, recv_sem=rsem,
            device_id=dev, device_id_type=MESH,
        )

    loads = []
    for k, (r, m) in enumerate(CHUNKS):
        rows = pl.ds(r, m)
        loads.append([
            pltpu.make_async_copy(src.at[rows], dst.at[rows], in_sem.at[k, n])
            for n, (src, dst) in enumerate(
                ((ti_hbm, raw_ti), (si_hbm, raw_si), (tt_hbm, raw_tt), (st_hbm, raw_st))
            )
        ])
    for group in loads:
        for copy in group:
            copy.start()
    barrier = pltpu.get_barrier_semaphore()
    for dev in (across, sibling, after, before):
        pl.semaphore_signal(barrier, inc=1, device_id=dev, device_id_type=MESH)

    def unit(raw, rows, out, at, keep=None):
        wide = raw[rows].astype(jnp.float32)
        inverse = lax.rsqrt(jnp.sum(wide * wide, axis=-1, keepdims=True) + 1e-06)
        out[at] = (wide * inverse).astype(jnp.bfloat16)
        if keep is not None:
            keep[rows] = inverse

    def prev_at(k):
        r, m = CHUNKS[k]
        return pl.ds(OWN_TEXT + 2 * r, m), pl.ds(OWN_TEXT + 2 * r + m, m)

    y_cp, z_cp, d_cp, f_cp = [], [], [], []
    for k, (r, m) in enumerate(CHUNKS):
        own = pl.ds(r, m)
        po, ps = prev_at(k)
        y_cp.append((
            remote(TI.at[own], TI.at[pl.ds(ROWS + r, m)], y_s.at[2 * k], y_r.at[2 * k], across),
            remote(SI.at[own], SI.at[pl.ds(ROWS + r, m)], y_s.at[2 * k + 1], y_r.at[2 * k + 1], across),
        ))
        z_cp.append((
            remote(TT.at[own], TT.at[po], z_s.at[2 * k], z_r.at[2 * k], after),
            remote(ST.at[own], ST.at[po], z_s.at[2 * k + 1], z_r.at[2 * k + 1], after),
        ))
        d_cp.append((
            remote(TT.at[own], TT.at[pl.ds(ROWS + r, m)], d_s.at[2 * k], d_r.at[2 * k], sibling),
            remote(ST.at[own], ST.at[pl.ds(ROWS + r, m)], d_s.at[2 * k + 1], d_r.at[2 * k + 1], sibling),
        ))
        f_cp.append((
            remote(TT.at[po], TT.at[ps], f_s.at[2 * k], f_r.at[2 * k], sibling),
            remote(ST.at[po], ST.at[ps], f_s.at[2 * k + 1], f_r.at[2 * k + 1], sibling),
        ))

    for k, (r, m) in enumerate(CHUNKS):
        own = pl.ds(r, m)
        for copy in loads[k]:
            copy.wait()
        unit(raw_ti, own, TI, own)
        unit(raw_tt, own, TT, own)
        if k == 0:
            pl.semaphore_wait(barrier, 4)
        y_cp[k][0].start()
        z_cp[k][0].start()
        unit(raw_si, own, SI, own, inv_i)
        unit(raw_st, own, ST, own, inv_t)
        y_cp[k][1].start()
        z_cp[k][1].start()
        d_cp[k][0].start()
        d_cp[k][1].start()

    def teach(i, m, j, n):
        dot = lax.dot_general(TI[pl.ds(i, m)], TT[pl.ds(j, n)], NT, preferred_element_type=jnp.float32)
        TG[pl.ds(i, m), pl.ds(j, n)] = jax.nn.sigmoid(t_scale * dot + t_bias)

    def study(i, m, j, n):
        dot = lax.dot_general(SI[pl.ds(i, m)], ST[pl.ds(j, n)], NT, preferred_element_type=jnp.float32)
        at = (pl.ds(i, m), pl.ds(j, n))
        W[at] = (jax.nn.sigmoid(s_scale * dot + s_bias) - TG[at]).astype(jnp.bfloat16)

    teach(0, ROWS, 0, ROWS)
    study(0, ROWS, 0, ROWS)
    for k in range(N_CH):
        for copy in d_cp[k]:
            copy.wait_recv()
    teach(0, ROWS, ROWS, ROWS)
    study(0, ROWS, ROWS, ROWS)

    for k, (r, m) in enumerate(CHUNKS):
        j = OWN_TEXT + 2 * r
        for half, tile in ((0, teach), (1, study)):
            z_cp[k][half].wait_recv()
            f_cp[k][half].start()
            y_cp[k][half].wait_recv()
            tile(ROWS + r, m, 0, j)
            f_cp[k][half].wait_recv()
            tile(0, ROWS + r + m, j, 2 * m)

    yp_cp = [
        remote(y_out.at[pl.ds(c * PULL, PULL)], y_in.at[pl.ds(c * PULL, PULL)], yp_s.at[c], yp_r.at[c], across)
        for c in range(N_PULL)
    ]
    zp_cp = [
        remote(z_out.at[pl.ds(r, m)], z_in.at[pl.ds(r, m)], zp_s.at[k], zp_r.at[k], before)
        for k, (r, m) in enumerate(CHUNKS)
    ]
    dp_cp = [
        remote(dp_out.at[pl.ds(r, m)], dp_in.at[pl.ds(r, m)], dp_s.at[k], dp_r.at[k], sibling)
        for k, (r, m) in enumerate(CHUNKS)
    ]
    dt_cp = remote(dt_out, dt_in, dt_s.at[0], dt_r.at[0], sibling)

    def image_pull(i, m):
        return jnp.dot(W[pl.ds(i, m), :], ST[...], preferred_element_type=jnp.float32)

    def text_pull(j, n):
        return lax.dot_general(W[:, pl.ds(j, n)], SI[...], TN, preferred_element_type=jnp.float32)

    def across_pull(c, n):
        y_out[pl.ds(c * PULL, n * PULL)] = image_pull(ROWS + c * PULL, n * PULL).astype(jnp.bfloat16)
        for i in range(c, c + n):
            yp_cp[i].start()

    def prev_pull(k):
        r, m = CHUNKS[k]
        pull = text_pull(OWN_TEXT + 2 * r, 2 * m)
        prev_own[pl.ds(r, m)] = pull[:m]
        dp_out[pl.ds(r, m)] = pull[m:].astype(jnp.bfloat16)
        dp_cp[k].start()

    def prev_send(k):
        r, m = CHUNKS[k]
        rows = pl.ds(r, m)
        dp_cp[k].wait_recv()
        z_out[rows] = (prev_own[rows] + dp_in[rows].astype(jnp.float32)).astype(jnp.bfloat16)
        zp_cp[k].start()

    across_pull(0, 2)
    prev_pull(0)
    across_pull(2, 4)
    prev_pull(1)
    prev_send(0)
    prev_pull(2)
    prev_send(1)
    prev_pull(3)
    prev_send(2)
    prev_send(3)
    dt_out[...] = text_pull(ROWS, ROWS).astype(jnp.bfloat16)
    dt_cp.start()
    img_own[...] = image_pull(0, ROWS)
    txt_own[...] = text_pull(0, ROWS)
    dt_cp.wait_recv()

    def project(pull, raw, inverse, scale):
        row = raw.astype(jnp.float32) * inverse
        grown = scale * pull
        return (grown - row * jnp.sum(row * grown, axis=-1, keepdims=True)) * inverse

    outs = []

    def finish_image(c):
        rows = pl.ds(c * PULL, PULL)
        yp_cp[c].wait_recv()
        pull = img_own[rows] + y_in[rows].astype(jnp.float32)
        gi_buf[rows] = project(pull, raw_si[rows], inv_i[rows], s_scale)
        outs.append(pltpu.make_async_copy(gi_buf.at[rows], gi_hbm.at[rows], out_sem.at[len(outs)]))
        outs[-1].start()

    def finish_text(k):
        r, m = CHUNKS[k]
        rows = pl.ds(r, m)
        zp_cp[k].wait_recv()
        pull = txt_own[rows] + dt_in[rows].astype(jnp.float32) + z_in[rows].astype(jnp.float32)
        gt_buf[rows] = project(pull, raw_st[rows], inv_t[rows], s_scale)
        outs.append(pltpu.make_async_copy(gt_buf.at[rows], gt_hbm.at[rows], out_sem.at[len(outs)]))
        outs[-1].start()

    for step in ((0,), (1,), (2, 0), (3,), (4, 1), (5, 2), (None, 3)):
        if step[0] is not None:
            finish_image(step[0])
        if len(step) > 1:
            finish_text(step[1])

    for group in (*y_cp, *z_cp, *d_cp, *f_cp, yp_cp, zp_cp, dp_cp, (dt_cp,)):
        for copy in group:
            copy.wait_send()
    for copy in outs:
        copy.wait()


def per_device(si, st, ti, tt, ss, sb, ts, tb):
    half, full = jnp.bfloat16, jnp.float32
    dma = pltpu.SemaphoreType.DMA
    smem = pl.BlockSpec(memory_space=pltpu.SMEM)
    hbm = pl.BlockSpec(memory_space=pl.ANY)
    part = lambda dtype: pltpu.VMEM((ROWS, D_S), dtype)
    return pl.pallas_call(
        kernel,
        out_shape=(jax.ShapeDtypeStruct((ROWS, D_S), full),) * 2,
        in_specs=[smem] * 4 + [hbm] * 4,
        out_specs=(hbm, hbm),
        scratch_shapes=[
            part(half), part(half), pltpu.VMEM((ROWS, D_T), half), pltpu.VMEM((ROWS, D_T), half),
            pltpu.VMEM((ROWS, 1), full), pltpu.VMEM((ROWS, 1), full),
            pltpu.VMEM((2 * ROWS, D_S), half), pltpu.VMEM((2 * ROWS, D_T), half),
            pltpu.VMEM((4 * ROWS, D_S), half), pltpu.VMEM((4 * ROWS, D_T), half),
            pltpu.VMEM((2 * ROWS, 4 * ROWS), full), pltpu.VMEM((2 * ROWS, 4 * ROWS), half),
            part(full), part(full), part(full),
            *[part(half)] * 8,
            part(full), part(full),
            dma((N_CH, 4)), dma((N_PULL + N_CH,)),
            *[dma((2 * N_CH,))] * 8,
            dma((N_PULL,)), dma((N_PULL,)), dma((1,)), dma((1,)),
            *[dma((N_CH,))] * 4,
        ],
        compiler_params=pltpu.CompilerParams(
            collective_id=0, has_side_effects=True, vmem_limit_bytes=56 * 2**20,
        ),
    )(ss, sb, ts, tb, si, st, ti, tt)


def solution(mesh):
    row = P(("loop", "grp"), None)
    return jax.shard_map(
        per_device,
        mesh=mesh,
        in_specs=(row, row, row, row, P(), P(), P(), P()),
        out_specs=(row, row),
        check_vma=False,
    )
```

time: 389 us -> 73.7 us (0.19)
  waiting for transfers between devices: 342 us -> 0 us
  Pallas kernels: 0 us -> 66.8 us
  matrix products: 18 us -> 0 us
  between operations: 16.5 us -> 3.23 us
  other arithmetic: 9.71 us -> 0 us
    ppermute x3 -> x0, waiting for transfers between devices: 149 us -> none  [shifted(): return lax.ppermute(block, axis, route)]
    all_gather x2 -> x0, waiting for transfers between devices: 146 us -> none  [the longest x1 99.8 us: per_device(): lax.all_gather(text_half, 'grp', axis=0, tiled=True)]
    pallas_call x0 -> x1, Pallas kernels: none -> 66.8 us  [per_device(): pl.pallas_call(kernel, out_shape=(jax.ShapeDtypeStruct((ROWS, D_S), full)...]
    reduce_scatter x1 -> x0, waiting for transfers between devices: 46.3 us -> none  [per_device(): lax.psum_scatter(carried, 'grp', scatter_dimension=0, tiled=True)]
    dot_general x8 -> x0, matrix products: 18 us -> none  [the longest x2 5.99 us: tile_terms(): jnp.einsum('id,jd->ij', teach_image, teach_block, preferred_element_type=...]
  transfers between devices with their start and end apart: 6 -> 0, of which waited for: 5 -> 0; matrix products, arithmetic and copies ran while one was open for 4% -> 0% of each run, Pallas kernels for 0% -> 0%
where the time goes in v1:
time: 73.7 us; the launch traced here: 73.5 us
  Pallas kernels  66.8 us (91%)
  local copies, waits for them, and re-layouts  3.47 us (5%)
  between operations  3.23 us (4%)
    pallas_call x1, Pallas kernels, per_device(): pl.pallas_call(kernel, out_shape=(jax.ShapeDtypeStruct((ROWS, D_S), full)...  66.8 us
    unnamed x4, local copies, waits for them, and re-layouts  3.47 us

profile of v1, /device:TPU:1, one launch (start us, length us, event | category | flops | bytes accessed | tf_op | source)
XLA Modules:
  0.0 73.5 jit_solution(2672790336091592079)
XLA Ops:
  3.2 66.8 %shard_map.95 = (f32[384,768]{1,0:T(8,128)}, f32[384,768]{1,0:T(8,128)}) custom-call(f32[1]{0:T(128)S(6)} %copy.12.ss_ref, f32[1]{0:T(128)S(6)} %copy.13.sb_ref, f32[1]{0:T(128)S(6)} %copy.14.ts_ref, f32[1]{0:T(128)S(6)} %copy.15.tb_ref, bf16[384,768]{1,0:T(8,128)(2,1)} %si_hbm.1, bf16[384,768]{1,0:T(8,128)(2,1)} %st_hbm.1, bf16[384,1152]{1,0:T(8,128)(2,1)} %ti_hbm.1, ...), custom_call_target="tpu_custom_call" | custom-call | tf_op jit(solution)/shard_map/pallas_call | solution.py:251
  70.1 0.0 copy-start
  70.1 2.5 %copy.16 = f32[384,768]{1,0:T(8,128)} copy(f32[384,768]{1,0:T(8,128)} %get-tuple-element.4) | data formatting | bytes 2359296
  72.5 0.0 copy-done
  72.5 1.0 %copy.17 = f32[384,768]{1,0:T(8,128)} copy(f32[384,768]{1,0:T(8,128)S(1)} %copy-done) | data formatting | bytes 2359296
Async XLA Ops:
  70.1 2.5 %copy-start = (f32[384,768]{1,0:T(8,128)S(1)}, f32[384,768]{1,0:T(8,128)}, u32[]{:S(2)}) copy-start(f32[384,768]{1,0:T(8,128)} %get-tuple-element.5) | copy-start | bytes 3538948

commit v2 on v1

--- a/solution.py
+++ b/solution.py
@@ -9,12 +9,16 @@
 
 MESH = pl.DeviceIdType.MESH
 N_LOOP = 64
-RUN = 8
+HOP = 3
+RUN = 2 * HOP + 2
 ROWS = 384
 D_S = 768
 D_T = 1152
 CHUNKS = ((0, 128), (128, 128), (256, 64), (320, 64))
 N_CH = len(CHUNKS)
+FAR = (2, 3)
+FAR_ROWS = 128
+N_WRITE = 4
 PULL = 64
 N_PULL = ROWS // PULL
 OWN_TEXT = 2 * ROWS
@@ -28,14 +32,18 @@
     grp = lax.axis_index("grp")
     chip = grp // 2
     core = grp % 2
-    seam_next = ((loop % RUN) + 1) // RUN
-    seam_prev = (((N_LOOP - loop) % RUN) + RUN - 1) // RUN
-    seam_prev = 1 - seam_prev
-    across = (loop, (1 - chip) * 2 + core)
+    place = loop % RUN
+    swapped = (1 - chip) * 2 + core
+
+    def at(step, swap):
+        side = jnp.where(swap, swapped, grp)
+        return ((loop + step + N_LOOP) % N_LOOP, side)
+
+    across = (loop, swapped)
     sibling = (loop, chip * 2 + 1 - core)
-    after = ((loop + 1) % N_LOOP, ((chip + seam_next) % 2) * 2 + core)
-    before = ((loop + N_LOOP - 1) % N_LOOP, ((chip + seam_prev) % 2) * 2 + core)
-    return across, sibling, after, before
+    after = at(1, place == RUN - 1)
+    before = at(-1, place == 0)
+    return place, across, sibling, after, before, at
 
 
 def kernel(
@@ -45,11 +53,13 @@
     img_own, txt_own, prev_own,
     y_out, y_in, dt_out, dt_in, dp_out, dp_in, z_out, z_in,
     gi_buf, gt_buf,
+    far_t, far_s,
     in_sem, out_sem,
+    q_s, q_r,
     y_s, y_r, z_s, z_r, d_s, d_r, f_s, f_r,
     yp_s, yp_r, dt_s, dt_r, dp_s, dp_r, zp_s, zp_r,
 ):
-    across, sibling, after, before = partners()
+    place, across, sibling, after, before, at = partners()
     s_scale, s_bias, t_scale, t_bias = ss_ref[0], sb_ref[0], ts_ref[0], tb_ref[0]
 
     def remote(src, dst, ssem, rsem, dev):
@@ -71,8 +81,22 @@
         for copy in group:
             copy.start()
     barrier = pltpu.get_barrier_semaphore()
-    for dev in (across, sibling, after, before):
+    for dev in (across, sibling, before):
         pl.semaphore_signal(barrier, inc=1, device_id=dev, device_id_type=MESH)
+    relays = place % HOP == 1
+
+    @pl.when(place == 1 + HOP)
+    def _():
+        pl.semaphore_signal(barrier, inc=1, device_id=at(HOP, False), device_id_type=MESH)
+
+    @pl.when(place == 1)
+    def _():
+        pl.semaphore_signal(barrier, inc=1, device_id=at(HOP - RUN, True), device_id_type=MESH)
+
+    @pl.when(place == 0)
+    def _():
+        pl.semaphore_signal(barrier, inc=1, device_id=at(1, False), device_id_type=MESH)
+
 
     def unit(raw, rows, out, at, keep=None):
         wide = raw[rows].astype(jnp.float32)
@@ -85,7 +109,7 @@
         r, m = CHUNKS[k]
         return pl.ds(OWN_TEXT + 2 * r, m), pl.ds(OWN_TEXT + 2 * r + m, m)
 
-    y_cp, z_cp, d_cp, f_cp = [], [], [], []
+    y_cp, z_cp, d_cp, f_cp, far_cp = [], [], [], [], []
     for k, (r, m) in enumerate(CHUNKS):
         own = pl.ds(r, m)
         po, ps = prev_at(k)
@@ -105,23 +129,78 @@
             remote(TT.at[po], TT.at[ps], f_s.at[2 * k], f_r.at[2 * k], sibling),
             remote(ST.at[po], ST.at[ps], f_s.at[2 * k + 1], f_r.at[2 * k + 1], sibling),
         ))
-
-    for k, (r, m) in enumerate(CHUNKS):
-        own = pl.ds(r, m)
-        for copy in loads[k]:
+        if k in FAR:
+            down, over, home = at(-HOP, False), at(RUN - HOP, True), at(-1, False)
+            stop = pl.ds(r - CHUNKS[FAR[0]][0], m)
+            pairs = []
+            for half, (text, stay) in enumerate(((TT, far_t), (ST, far_s))):
+                n = 2 * (k - FAR[0]) + half
+                pairs.append((
+                    remote(text.at[own], stay.at[stop], q_s.at[n], q_r.at[n], down),
+                    remote(stay.at[stop], stay.at[stop], q_s.at[n], q_r.at[n], over),
+                    remote(stay.at[stop], text.at[po], q_s.at[n], z_r.at[2 * k + half], home),
+                ))
+            far_cp.extend(pairs)
+
+    def pass_on(hop, first, last):
+        @pl.when(place == 1 + HOP * (2 - hop))
+        def _():
+            for n in range(first, last):
+                far_cp[n][0].wait_recv()
+                far_cp[n][hop].start()
+
+    def prepare_images(k):
+        own = pl.ds(*CHUNKS[k])
+        unit(raw_ti, own, TI, own)
+        y_cp[k][0].start()
+        unit(raw_si, own, SI, own, inv_i)
+        y_cp[k][1].start()
+
+    def prepare_text(k):
+        own = pl.ds(*CHUNKS[k])
+        unit(raw_tt, own, TT, own)
+        unit(raw_st, own, ST, own, inv_t)
+
+    for copy in loads[0]:
+        copy.wait()
+    own = pl.ds(*CHUNKS[0])
+    unit(raw_ti, own, TI, own)
+    unit(raw_tt, own, TT, own)
+    pl.semaphore_wait(barrier, jnp.where(relays, 4, 3))
+    y_cp[0][0].start()
+    z_cp[0][0].start()
+    unit(raw_si, own, SI, own, inv_i)
+    unit(raw_st, own, ST, own, inv_t)
+    y_cp[0][1].start()
+    z_cp[0][1].start()
+    d_cp[0][0].start()
+    d_cp[0][1].start()
+    for group in loads[1:]:
+        for copy in group:
             copy.wait()
-        unit(raw_ti, own, TI, own)
-        unit(raw_tt, own, TT, own)
-        if k == 0:
-            pl.semaphore_wait(barrier, 4)
-        y_cp[k][0].start()
-        z_cp[k][0].start()
-        unit(raw_si, own, SI, own, inv_i)
-        unit(raw_st, own, ST, own, inv_t)
-        y_cp[k][1].start()
-        z_cp[k][1].start()
-        d_cp[k][0].start()
-        d_cp[k][1].start()
+    for k in FAR:
+        prepare_text(k)
+
+        @pl.when(place == RUN - 1)
+        def _():
+            for half in (0, 1):
+                far_cp[2 * (k - FAR[0]) + half][0].start()
+    for k in range(1, N_CH):
+        if k not in FAR:
+            prepare_text(k)
+            for half in (0, 1):
+                z_cp[k][half].start()
+        for half in (0, 1):
+            d_cp[k][half].start()
+
+    @pl.when(place != RUN - 1)
+    def _():
+        for k in FAR:
+            for half in (0, 1):
+                z_cp[k][half].start()
+
+    for k in range(1, N_CH):
+        prepare_images(k)
 
     def teach(i, m, j, n):
         dot = lax.dot_general(TI[pl.ds(i, m)], TT[pl.ds(j, n)], NT, preferred_element_type=jnp.float32)
@@ -140,6 +219,7 @@
     teach(0, ROWS, ROWS, ROWS)
     study(0, ROWS, ROWS, ROWS)
 
+    pass_on(1, 0, 3)
     for k, (r, m) in enumerate(CHUNKS):
         j = OWN_TEXT + 2 * r
         for half, tile in ((0, teach), (1, study)):
@@ -149,6 +229,11 @@
             tile(ROWS + r, m, 0, j)
             f_cp[k][half].wait_recv()
             tile(0, ROWS + r + m, j, 2 * m)
+        if k == 0:
+            pass_on(1, 3, 4)
+            pass_on(2, 0, 2)
+        if k == 1:
+            pass_on(2, 2, 4)
 
     yp_cp = [
         remote(y_out.at[pl.ds(c * PULL, PULL)], y_in.at[pl.ds(c * PULL, PULL)], yp_s.at[c], yp_r.at[c], across)
@@ -235,20 +320,46 @@
         if len(step) > 1:
             finish_text(step[1])
 
-    for group in (*y_cp, *z_cp, *d_cp, *f_cp, yp_cp, zp_cp, dp_cp, (dt_cp,)):
+    for n, copies in enumerate(far_cp):
+        @pl.when(relays)
+        def _():
+            copies[0].wait_send()
+
+        @pl.when(place != RUN - 1)
+        def _():
+            z_cp[FAR[n // 2]][n % 2].wait_send()
+
+    near = [z_cp[k] for k in range(N_CH) if k not in FAR]
+    for group in (*y_cp, *near, *d_cp, *f_cp, yp_cp, zp_cp, dp_cp, (dt_cp,)):
         for copy in group:
             copy.wait_send()
     for copy in outs:
         copy.wait()
 
 
+def write_kernel(gi_hbm, gt_hbm, gi_out, gt_out, gi_buf, gt_buf, in_sem, out_sem):
+    reads, writes = [], []
+    for k in range(N_WRITE):
+        rows = pl.ds(k * (ROWS // N_WRITE), ROWS // N_WRITE)
+        for n, (src, buf, dst) in enumerate(((gi_hbm, gi_buf, gi_out), (gt_hbm, gt_buf, gt_out))):
+            reads.append(pltpu.make_async_copy(src.at[rows], buf.at[rows], in_sem.at[k, n]))
+            writes.append(pltpu.make_async_copy(buf.at[rows], dst.at[rows], out_sem.at[k, n]))
+    for copy in reads:
+        copy.start()
+    for read, write in zip(reads, writes):
+        read.wait()
+        write.start()
+    for copy in writes:
+        copy.wait()
+
+
 def per_device(si, st, ti, tt, ss, sb, ts, tb):
     half, full = jnp.bfloat16, jnp.float32
     dma = pltpu.SemaphoreType.DMA
     smem = pl.BlockSpec(memory_space=pltpu.SMEM)
-    hbm = pl.BlockSpec(memory_space=pl.ANY)
+    hbm = pl.BlockSpec(memory_space=pltpu.HBM)
     part = lambda dtype: pltpu.VMEM((ROWS, D_S), dtype)
-    return pl.pallas_call(
+    grads = pl.pallas_call(
         kernel,
         out_shape=(jax.ShapeDtypeStruct((ROWS, D_S), full),) * 2,
         in_specs=[smem] * 4 + [hbm] * 4,
@@ -262,7 +373,9 @@
             part(full), part(full), part(full),
             *[part(half)] * 8,
             part(full), part(full),
+            pltpu.VMEM((FAR_ROWS, D_T), half), pltpu.VMEM((FAR_ROWS, D_S), half),
             dma((N_CH, 4)), dma((N_PULL + N_CH,)),
+            dma((2 * len(FAR),)), dma((2 * len(FAR),)),
             *[dma((2 * N_CH,))] * 8,
             dma((N_PULL,)), dma((N_PULL,)), dma((1,)), dma((1,)),
             *[dma((N_CH,))] * 4,
@@ -271,6 +384,14 @@
             collective_id=0, has_side_effects=True, vmem_limit_bytes=56 * 2**20,
         ),
     )(ss, sb, ts, tb, si, st, ti, tt)
+    return pl.pallas_call(
+        write_kernel,
+        out_shape=(jax.ShapeDtypeStruct((ROWS, D_S), full),) * 2,
+        in_specs=[hbm, hbm],
+        out_specs=(hbm, hbm),
+        scratch_shapes=[part(full), part(full), dma((N_WRITE, 2)), dma((N_WRITE, 2))],
+        compiler_params=pltpu.CompilerParams(vmem_limit_bytes=56 * 2**20),
+    )(*grads)
 
 
 def solution(mesh):

time: 73.7 us -> 67.8 us (0.920)
  local copies, waits for them, and re-layouts: 3.47 us -> 0 us
  Pallas kernels: 66.8 us -> 64.2 us
    pallas_call x1, Pallas kernels: 66.8 us -> 61.8 us  [per_device(): pl.pallas_call(kernel, out_shape=(jax.ShapeDtypeStruct((ROWS, D_S), full)...]
    unnamed x4 -> x0, local copies, waits for them, and re-layouts: 3.47 us -> none
    pallas_call x0 -> x1, Pallas kernels: none -> 2.49 us  [per_device(): pl.pallas_call(write_kernel, out_shape=(jax.ShapeDtypeStruct((ROWS, D_S),...]
where the time goes in v2:
time: 67.8 us; the launch traced here: 67.6 us
  Pallas kernels  64.2 us (95%)
  between operations  3.38 us (5%)
    pallas_call x1, Pallas kernels, per_device(): pl.pallas_call(kernel, out_shape=(jax.ShapeDtypeStruct((ROWS, D_S), full)...  61.8 us
    pallas_call x1, Pallas kernels, per_device(): pl.pallas_call(write_kernel, out_shape=(jax.ShapeDtypeStruct((ROWS, D_S),...  2.49 us

profile of v2, /device:TPU:1, one launch (start us, length us, event | category | flops | bytes accessed | tf_op | source)
XLA Modules:
  0.0 67.6 jit_solution(17117072959544829713)
XLA Ops:
  3.2 61.8 %shard_map.95 = (f32[384,768]{1,0:T(8,128)}, f32[384,768]{1,0:T(8,128)}) custom-call(f32[1]{0:T(128)S(6)} %copy.10.ss_ref, f32[1]{0:T(128)S(6)} %copy.11.sb_ref, f32[1]{0:T(128)S(6)} %copy.12.ts_ref, f32[1]{0:T(128)S(6)} %copy.13.tb_ref, bf16[384,768]{1,0:T(8,128)(2,1)} %si_hbm.1, bf16[384,768]{1,0:T(8,128)(2,1)} %st_hbm.1, bf16[384,1152]{1,0:T(8,128)(2,1)} %ti_hbm.1, ...), custom_call_target="tpu_custom_call" | custom-call | tf_op jit(solution)/shard_map/pallas_call | solution.py:362
  65.0 2.5 %shard_map.96 = (f32[384,768]{1,0:T(8,128)}, f32[384,768]{1,0:T(8,128)}) custom-call(f32[384,768]{1,0:T(8,128)} %get-tuple-element.4.gi_hbm, f32[384,768]{1,0:T(8,128)} %get-tuple-element.5.gt_hbm), custom_call_target="tpu_custom_call" | custom-call | tf_op jit(solution)/shard_map/pallas_call | solution.py:387

commit v3 on v2

--- a/solution.py
+++ b/solution.py
@@ -14,10 +14,12 @@
 ROWS = 384
 D_S = 768
 D_T = 1152
-CHUNKS = ((0, 128), (128, 128), (256, 64), (320, 64))
+CHUNKS = ((0, 64), (64, 128), (192, 64), (256, 64), (320, 64))
 N_CH = len(CHUNKS)
-FAR = (2, 3)
+FAR = (3, 4)
 FAR_ROWS = 128
+SPLIT = 2
+RELAY = ((1, 1, 1, 4), (1, 2, 0, 1), (2, 2, 1, 2), (3, 2, 2, 4))
 N_WRITE = 4
 PULL = 64
 N_PULL = ROWS // PULL
@@ -179,11 +181,12 @@
         for copy in group:
             copy.wait()
     for k in FAR:
-        prepare_text(k)
-
-        @pl.when(place == RUN - 1)
-        def _():
-            for half in (0, 1):
+        own = pl.ds(*CHUNKS[k])
+        for half, norm in ((0, (raw_tt, own, TT, own)), (1, (raw_st, own, ST, own, inv_t))):
+            unit(*norm)
+
+            @pl.when(place == RUN - 1)
+            def _():
                 far_cp[2 * (k - FAR[0]) + half][0].start()
     for k in range(1, N_CH):
         if k not in FAR:
@@ -219,21 +222,24 @@
     teach(0, ROWS, ROWS, ROWS)
     study(0, ROWS, ROWS, ROWS)
 
-    pass_on(1, 0, 3)
-    for k, (r, m) in enumerate(CHUNKS):
+    def arrive(k, half):
+        z_cp[k][half].wait_recv()
+        f_cp[k][half].start()
+
+    def step(k):
+        r, m = CHUNKS[k]
         j = OWN_TEXT + 2 * r
         for half, tile in ((0, teach), (1, study)):
-            z_cp[k][half].wait_recv()
-            f_cp[k][half].start()
+            arrive(k, half)
             y_cp[k][half].wait_recv()
+            if k == N_CH - 1 and half == 1:
+                break
             tile(ROWS + r, m, 0, j)
             f_cp[k][half].wait_recv()
             tile(0, ROWS + r + m, j, 2 * m)
-        if k == 0:
-            pass_on(1, 3, 4)
-            pass_on(2, 0, 2)
-        if k == 1:
-            pass_on(2, 2, 4)
+        for when, hop, first, last in RELAY:
+            if when == k + 1:
+                pass_on(hop, first, last)
 
     yp_cp = [
         remote(y_out.at[pl.ds(c * PULL, PULL)], y_in.at[pl.ds(c * PULL, PULL)], yp_s.at[c], yp_r.at[c], across)
@@ -260,12 +266,15 @@
         for i in range(c, c + n):
             yp_cp[i].start()
 
-    def prev_pull(k):
-        r, m = CHUNKS[k]
-        pull = text_pull(OWN_TEXT + 2 * r, 2 * m)
-        prev_own[pl.ds(r, m)] = pull[:m]
-        dp_out[pl.ds(r, m)] = pull[m:].astype(jnp.bfloat16)
-        dp_cp[k].start()
+    def prev_pull(first, last):
+        r, rows = CHUNKS[first][0], sum(m for _, m in CHUNKS[first:last])
+        pull = text_pull(OWN_TEXT + 2 * r, 2 * rows)
+        for k in range(first, last):
+            at, m = CHUNKS[k]
+            mine = 2 * (at - r)
+            prev_own[pl.ds(at, m)] = pull[mine:mine + m]
+            dp_out[pl.ds(at, m)] = pull[mine + m:mine + 2 * m].astype(jnp.bfloat16)
+            dp_cp[k].start()
 
     def prev_send(k):
         r, m = CHUNKS[k]
@@ -274,16 +283,57 @@
         z_out[rows] = (prev_own[rows] + dp_in[rows].astype(jnp.float32)).astype(jnp.bfloat16)
         zp_cp[k].start()
 
+    @pl.when(place != 0)
+    def _():
+        pass_on(1, 0, 1)
+        for k in range(N_CH):
+            step(k)
+        r, m = CHUNKS[-1]
+        j = OWN_TEXT + 2 * r
+        study(ROWS + r, m, OWN_TEXT, j - OWN_TEXT)
+        prev_pull(0, 1)
+        study(ROWS + r, m, 0, OWN_TEXT)
+        f_cp[N_CH - 1][1].wait_recv()
+        study(0, 2 * ROWS, j, 2 * m)
+
+    @pl.when(place == 0)
+    def _():
+        last = N_CH - 1
+        r, m = CHUNKS[last]
+        mid = CHUNKS[SPLIT][0]
+        j = OWN_TEXT + 2 * mid
+        for k in range(last):
+            for half, tile in ((0, teach), (1, study)):
+                y_cp[k][half].wait_recv()
+                tile(ROWS + CHUNKS[k][0], CHUNKS[k][1], 0, OWN_TEXT)
+            if k == 1:
+                arrive(0, 0)
+                arrive(0, 1)
+        for k in (*range(1, SPLIT), *FAR[:-1]):
+            arrive(k, 0)
+            arrive(k, 1)
+        for half, tile in ((0, teach), (1, study)):
+            for k in range(SPLIT):
+                f_cp[k][half].wait_recv()
+            tile(0, ROWS + r, OWN_TEXT, j - OWN_TEXT)
+        for half, tile in ((0, teach), (1, study)):
+            for k in (*range(SPLIT, FAR[0]), last):
+                arrive(k, half)
+            y_cp[last][half].wait_recv()
+            tile(ROWS + r, m, 0, j)
+            for k in range(SPLIT, N_CH):
+                f_cp[k][half].wait_recv()
+            tile(0, 2 * ROWS, j, 2 * (ROWS - mid))
+        prev_pull(0, 1)
+
     across_pull(0, 2)
-    prev_pull(0)
+    prev_send(0)
+    prev_pull(1, 2)
     across_pull(2, 4)
-    prev_pull(1)
-    prev_send(0)
-    prev_pull(2)
     prev_send(1)
-    prev_pull(3)
-    prev_send(2)
-    prev_send(3)
+    prev_pull(2, N_CH)
+    for k in range(2, N_CH):
+        prev_send(k)
     dt_out[...] = text_pull(ROWS, ROWS).astype(jnp.bfloat16)
     dt_cp.start()
     img_own[...] = image_pull(0, ROWS)
@@ -314,11 +364,10 @@
         outs.append(pltpu.make_async_copy(gt_buf.at[rows], gt_hbm.at[rows], out_sem.at[len(outs)]))
         outs[-1].start()
 
-    for step in ((0,), (1,), (2, 0), (3,), (4, 1), (5, 2), (None, 3)):
-        if step[0] is not None:
-            finish_image(step[0])
-        if len(step) > 1:
-            finish_text(step[1])
+    for image, text in ((0, 0), (1, None), (2, 1), (3, 2), (4, 3), (5, 4)):
+        finish_image(image)
+        if text is not None:
+            finish_text(text)
 
     for n, copies in enumerate(far_cp):
         @pl.when(relays)

time: 67.8 us -> 65.2 us (0.962)
  Pallas kernels: 64.2 us -> 61.6 us
    pallas_call x1, Pallas kernels: 61.8 us -> 59.1 us  [per_device(): pl.pallas_call(kernel, out_shape=(jax.ShapeDtypeStruct((ROWS, D_S), full)...]
where the time goes in v3:
time: 65.2 us; the launch traced here: 65 us
  Pallas kernels  61.6 us (94%)
  between operations  3.38 us (5%)
    pallas_call x1, Pallas kernels, per_device(): pl.pallas_call(kernel, out_shape=(jax.ShapeDtypeStruct((ROWS, D_S), full)...  59.1 us
    pallas_call x1, Pallas kernels, per_device(): pl.pallas_call(write_kernel, out_shape=(jax.ShapeDtypeStruct((ROWS, D_S),...  2.49 us

profile of v3, /device:TPU:1, one launch (start us, length us, event | category | flops | bytes accessed | tf_op | source)
XLA Modules:
  0.0 65.0 jit_solution(5368382133245030272)
XLA Ops:
  3.2 59.1 %shard_map.95 = (f32[384,768]{1,0:T(8,128)}, f32[384,768]{1,0:T(8,128)}) custom-call(f32[1]{0:T(128)S(6)} %copy.10.ss_ref, f32[1]{0:T(128)S(6)} %copy.11.sb_ref, f32[1]{0:T(128)S(6)} %copy.12.ts_ref, f32[1]{0:T(128)S(6)} %copy.13.tb_ref, bf16[384,768]{1,0:T(8,128)(2,1)} %si_hbm.1, bf16[384,768]{1,0:T(8,128)(2,1)} %st_hbm.1, bf16[384,1152]{1,0:T(8,128)(2,1)} %ti_hbm.1, ...), custom_call_target="tpu_custom_call" | custom-call | tf_op jit(solution)/shard_map/pallas_call | solution.py:411
  62.4 2.5 %shard_map.96 = (f32[384,768]{1,0:T(8,128)}, f32[384,768]{1,0:T(8,128)}) custom-call(f32[384,768]{1,0:T(8,128)} %get-tuple-element.4.gi_hbm, f32[384,768]{1,0:T(8,128)} %get-tuple-element.5.gt_hbm), custom_call_target="tpu_custom_call" | custom-call | tf_op jit(solution)/shard_map/pallas_call | solution.py:436

commit v4 on v3

--- a/solution.py
+++ b/solution.py
@@ -20,8 +20,9 @@
 FAR_ROWS = 128
 SPLIT = 2
 RELAY = ((1, 1, 1, 4), (1, 2, 0, 1), (2, 2, 1, 2), (3, 2, 2, 4))
-N_WRITE = 4
+N_WRITE = 2
 PULL = 64
+FIRST = 2 * PULL
 N_PULL = ROWS // PULL
 OWN_TEXT = 2 * ROWS
 
@@ -49,14 +50,13 @@
 
 
 def kernel(
-    ss_ref, sb_ref, ts_ref, tb_ref, si_hbm, st_hbm, ti_hbm, tt_hbm, gi_hbm, gt_hbm,
+    ss_ref, sb_ref, ts_ref, tb_ref, si_hbm, st_hbm, ti_hbm, tt_hbm, gi_ref, gt_ref,
     raw_si, raw_st, raw_ti, raw_tt, inv_i, inv_t,
     SI, TI, ST, TT, TG, W,
     img_own, txt_own, prev_own,
     y_out, y_in, dt_out, dt_in, dp_out, dp_in, z_out, z_in,
-    gi_buf, gt_buf,
     far_t, far_s,
-    in_sem, out_sem,
+    in_sem,
     q_s, q_r,
     y_s, y_r, z_s, z_r, d_s, d_r, f_s, f_r,
     yp_s, yp_r, dt_s, dt_r, dp_s, dp_r, zp_s, zp_r,
@@ -266,9 +266,28 @@
         for i in range(c, c + n):
             yp_cp[i].start()
 
-    def prev_pull(first, last):
-        r, rows = CHUNKS[first][0], sum(m for _, m in CHUNKS[first:last])
-        pull = text_pull(OWN_TEXT + 2 * r, 2 * rows)
+    def early_across(j):
+        gi_ref[pl.ds(0, FIRST)] = jnp.dot(
+            W[pl.ds(ROWS, FIRST), pl.ds(0, j)], ST[pl.ds(0, j)], preferred_element_type=jnp.float32
+        )
+
+    def late_across(j):
+        rest = jnp.dot(
+            W[pl.ds(ROWS, FIRST), pl.ds(j, 4 * ROWS - j)], ST[pl.ds(j, 4 * ROWS - j)],
+            preferred_element_type=jnp.float32,
+        )
+        y_out[pl.ds(0, FIRST)] = (gi_ref[pl.ds(0, FIRST)] + rest).astype(jnp.bfloat16)
+        for i in range(FIRST // PULL):
+            yp_cp[i].start()
+
+    def first_text(i, m):
+        m0 = CHUNKS[0][1]
+        return lax.dot_general(
+            W[pl.ds(i, m), pl.ds(OWN_TEXT, 2 * m0)], SI[pl.ds(i, m)], TN, preferred_element_type=jnp.float32
+        )
+
+    def prev_leave(pull, first, last):
+        r = CHUNKS[first][0]
         for k in range(first, last):
             at, m = CHUNKS[k]
             mine = 2 * (at - r)
@@ -276,6 +295,10 @@
             dp_out[pl.ds(at, m)] = pull[mine + m:mine + 2 * m].astype(jnp.bfloat16)
             dp_cp[k].start()
 
+    def prev_pull(first, last):
+        r, rows = CHUNKS[first][0], sum(m for _, m in CHUNKS[first:last])
+        prev_leave(text_pull(OWN_TEXT + 2 * r, 2 * rows), first, last)
+
     def prev_send(k):
         r, m = CHUNKS[k]
         rows = pl.ds(r, m)
@@ -286,15 +309,21 @@
     @pl.when(place != 0)
     def _():
         pass_on(1, 0, 1)
-        for k in range(N_CH):
+        last = N_CH - 1
+        for k in range(last):
             step(k)
-        r, m = CHUNKS[-1]
+        r, m = CHUNKS[last]
         j = OWN_TEXT + 2 * r
+        early = pl.ds(0, 2 * CHUNKS[0][1])
+        gt_ref[early] = first_text(0, ROWS + r)
+        early_across(j)
+        step(last)
         study(ROWS + r, m, OWN_TEXT, j - OWN_TEXT)
-        prev_pull(0, 1)
+        prev_leave(gt_ref[early] + first_text(ROWS + r, m), 0, 1)
         study(ROWS + r, m, 0, OWN_TEXT)
-        f_cp[N_CH - 1][1].wait_recv()
+        f_cp[last][1].wait_recv()
         study(0, 2 * ROWS, j, 2 * m)
+        late_across(j)
 
     @pl.when(place == 0)
     def _():
@@ -316,17 +345,19 @@
             for k in range(SPLIT):
                 f_cp[k][half].wait_recv()
             tile(0, ROWS + r, OWN_TEXT, j - OWN_TEXT)
+        early_across(j)
         for half, tile in ((0, teach), (1, study)):
             for k in (*range(SPLIT, FAR[0]), last):
                 arrive(k, half)
             y_cp[last][half].wait_recv()
             tile(ROWS + r, m, 0, j)
+            if half == 1:
+                prev_pull(0, 1)
             for k in range(SPLIT, N_CH):
                 f_cp[k][half].wait_recv()
             tile(0, 2 * ROWS, j, 2 * (ROWS - mid))
-        prev_pull(0, 1)
-
-    across_pull(0, 2)
+        late_across(j)
+
     prev_send(0)
     prev_pull(1, 2)
     across_pull(2, 4)
@@ -345,24 +376,18 @@
         grown = scale * pull
         return (grown - row * jnp.sum(row * grown, axis=-1, keepdims=True)) * inverse
 
-    outs = []
-
     def finish_image(c):
         rows = pl.ds(c * PULL, PULL)
         yp_cp[c].wait_recv()
         pull = img_own[rows] + y_in[rows].astype(jnp.float32)
-        gi_buf[rows] = project(pull, raw_si[rows], inv_i[rows], s_scale)
-        outs.append(pltpu.make_async_copy(gi_buf.at[rows], gi_hbm.at[rows], out_sem.at[len(outs)]))
-        outs[-1].start()
+        gi_ref[rows] = project(pull, raw_si[rows], inv_i[rows], s_scale)
 
     def finish_text(k):
         r, m = CHUNKS[k]
         rows = pl.ds(r, m)
         zp_cp[k].wait_recv()
         pull = txt_own[rows] + dt_in[rows].astype(jnp.float32) + z_in[rows].astype(jnp.float32)
-        gt_buf[rows] = project(pull, raw_st[rows], inv_t[rows], s_scale)
-        outs.append(pltpu.make_async_copy(gt_buf.at[rows], gt_hbm.at[rows], out_sem.at[len(outs)]))
-        outs[-1].start()
+        gt_ref[rows] = project(pull, raw_st[rows], inv_t[rows], s_scale)
 
     for image, text in ((0, 0), (1, None), (2, 1), (3, 2), (4, 3), (5, 4)):
         finish_image(image)
@@ -382,23 +407,17 @@
     for group in (*y_cp, *near, *d_cp, *f_cp, yp_cp, zp_cp, dp_cp, (dt_cp,)):
         for copy in group:
             copy.wait_send()
-    for copy in outs:
-        copy.wait()
-
-
-def write_kernel(gi_hbm, gt_hbm, gi_out, gt_out, gi_buf, gt_buf, in_sem, out_sem):
-    reads, writes = [], []
+
+
+def write_kernel(gi_ref, gt_ref, gi_hbm, gt_hbm, sem):
+    copies = []
     for k in range(N_WRITE):
         rows = pl.ds(k * (ROWS // N_WRITE), ROWS // N_WRITE)
-        for n, (src, buf, dst) in enumerate(((gi_hbm, gi_buf, gi_out), (gt_hbm, gt_buf, gt_out))):
-            reads.append(pltpu.make_async_copy(src.at[rows], buf.at[rows], in_sem.at[k, n]))
-            writes.append(pltpu.make_async_copy(buf.at[rows], dst.at[rows], out_sem.at[k, n]))
-    for copy in reads:
+        for n, (src, dst) in enumerate(((gi_ref, gi_hbm), (gt_ref, gt_hbm))):
+            copies.append(pltpu.make_async_copy(src.at[rows], dst.at[rows], sem.at[k, n]))
+    for copy in copies:
         copy.start()
-    for read, write in zip(reads, writes):
-        read.wait()
-        write.start()
-    for copy in writes:
+    for copy in copies:
         copy.wait()
 
 
@@ -407,12 +426,13 @@
     dma = pltpu.SemaphoreType.DMA
     smem = pl.BlockSpec(memory_space=pltpu.SMEM)
     hbm = pl.BlockSpec(memory_space=pltpu.HBM)
+    free = pl.BlockSpec(memory_space=pl.ANY)
     part = lambda dtype: pltpu.VMEM((ROWS, D_S), dtype)
     grads = pl.pallas_call(
         kernel,
         out_shape=(jax.ShapeDtypeStruct((ROWS, D_S), full),) * 2,
         in_specs=[smem] * 4 + [hbm] * 4,
-        out_specs=(hbm, hbm),
+        out_specs=(pl.BlockSpec(memory_space=pltpu.VMEM),) * 2,
         scratch_shapes=[
             part(half), part(half), pltpu.VMEM((ROWS, D_T), half), pltpu.VMEM((ROWS, D_T), half),
             pltpu.VMEM((ROWS, 1), full), pltpu.VMEM((ROWS, 1), full),
@@ -421,25 +441,24 @@
             pltpu.VMEM((2 * ROWS, 4 * ROWS), full), pltpu.VMEM((2 * ROWS, 4 * ROWS), half),
             part(full), part(full), part(full),
             *[part(half)] * 8,
-            part(full), part(full),
             pltpu.VMEM((FAR_ROWS, D_T), half), pltpu.VMEM((FAR_ROWS, D_S), half),
-            dma((N_CH, 4)), dma((N_PULL + N_CH,)),
+            dma((N_CH, 4)),
             dma((2 * len(FAR),)), dma((2 * len(FAR),)),
             *[dma((2 * N_CH,))] * 8,
             dma((N_PULL,)), dma((N_PULL,)), dma((1,)), dma((1,)),
             *[dma((N_CH,))] * 4,
         ],
         compiler_params=pltpu.CompilerParams(
-            collective_id=0, has_side_effects=True, vmem_limit_bytes=56 * 2**20,
+            collective_id=0, has_side_effects=True, vmem_limit_bytes=44 * 2**20,
         ),
-    )(ss, sb, ts, tb, si, st, ti, tt)
+    )(ss, sb, ts, tb, *[pltpu.with_memory_space_constraint(x, pltpu.HBM) for x in (si, st, ti, tt)])
     return pl.pallas_call(
         write_kernel,
         out_shape=(jax.ShapeDtypeStruct((ROWS, D_S), full),) * 2,
-        in_specs=[hbm, hbm],
+        in_specs=[free, free],
         out_specs=(hbm, hbm),
-        scratch_shapes=[part(full), part(full), dma((N_WRITE, 2)), dma((N_WRITE, 2))],
-        compiler_params=pltpu.CompilerParams(vmem_limit_bytes=56 * 2**20),
+        scratch_shapes=[dma((N_WRITE, 2))],
+        compiler_params=pltpu.CompilerParams(vmem_limit_bytes=2**20),
     )(*grads)
 
 

time: 65.2 us -> 63.3 us (0.971)
  Pallas kernels: 61.6 us -> 59.7 us
    pallas_call x1, Pallas kernels: 2.49 us -> 1.43 us  [per_device(): pl.pallas_call(write_kernel, out_shape=(jax.ShapeDtypeStruct((ROWS, D_S),...]
    pallas_call x1, Pallas kernels: 59.1 us -> 58.3 us  [per_device(): pl.pallas_call(kernel, out_shape=(jax.ShapeDtypeStruct((ROWS, D_S), full)...]
where the time goes in v4:
time: 63.3 us; the launch traced here: 63.1 us
  Pallas kernels  59.7 us (94%)
  between operations  3.4 us (5%)
    pallas_call x1, Pallas kernels, per_device(): pl.pallas_call(kernel, out_shape=(jax.ShapeDtypeStruct((ROWS, D_S), full)...  58.3 us
    pallas_call x1, Pallas kernels, per_device(): pl.pallas_call(write_kernel, out_shape=(jax.ShapeDtypeStruct((ROWS, D_S),...  1.43 us

profile of v4, /device:TPU:1, one launch (start us, length us, event | category | flops | bytes accessed | tf_op | source)
XLA Modules:
  0.0 63.1 jit_solution(4337669745159938962)
XLA Ops:
  3.2 58.3 %shard_map.95 = (f32[384,768]{1,0:T(8,128)S(1)}, f32[384,768]{1,0:T(8,128)S(1)}) custom-call(f32[1]{0:T(128)S(6)} %copy.10.ss_ref, f32[1]{0:T(128)S(6)} %copy.11.sb_ref, f32[1]{0:T(128)S(6)} %copy.12.ts_ref, f32[1]{0:T(128)S(6)} %copy.13.tb_ref, bf16[384,768]{1,0:T(8,128)(2,1)} %si_hbm.1, bf16[384,768]{1,0:T(8,128)(2,1)} %st_hbm.1, ...), custom_call_target="tpu_custom_call" | custom-call | tf_op jit(solution)/shard_map/pallas_call | solution.py:431
  61.5 1.4 %shard_map.96 = (f32[384,768]{1,0:T(8,128)}, f32[384,768]{1,0:T(8,128)}) custom-call(f32[384,768]{1,0:T(8,128)S(1)} %get-tuple-element.4.gi_ref, f32[384,768]{1,0:T(8,128)S(1)} %get-tuple-element.5.gt_ref), custom_call_target="tpu_custom_call" | custom-call | tf_op jit(solution)/shard_map/pallas_call | solution.py:455

commit v5 on v4

--- a/solution.py
+++ b/solution.py
@@ -46,7 +46,7 @@
     sibling = (loop, chip * 2 + 1 - core)
     after = at(1, place == RUN - 1)
     before = at(-1, place == 0)
-    return place, across, sibling, after, before, at
+    return core, place, across, sibling, after, before, at
 
 
 def kernel(
@@ -56,12 +56,12 @@
     img_own, txt_own, prev_own,
     y_out, y_in, dt_out, dt_in, dp_out, dp_in, z_out, z_in,
     far_t, far_s,
-    in_sem,
+    gate, in_sem,
     q_s, q_r,
     y_s, y_r, z_s, z_r, d_s, d_r, f_s, f_r,
     yp_s, yp_r, dt_s, dt_r, dp_s, dp_r, zp_s, zp_r,
 ):
-    place, across, sibling, after, before, at = partners()
+    core, place, across, sibling, after, before, at = partners()
     s_scale, s_bias, t_scale, t_bias = ss_ref[0], sb_ref[0], ts_ref[0], tb_ref[0]
 
     def remote(src, dst, ssem, rsem, dev):
@@ -70,35 +70,52 @@
             device_id=dev, device_id_type=MESH,
         )
 
-    loads = []
-    for k, (r, m) in enumerate(CHUNKS):
-        rows = pl.ds(r, m)
-        loads.append([
-            pltpu.make_async_copy(src.at[rows], dst.at[rows], in_sem.at[k, n])
+    loads = [
+        [
+            pltpu.make_async_copy(src.at[pl.ds(r, m)], dst.at[pl.ds(r, m)], in_sem.at[k, n])
             for n, (src, dst) in enumerate(
-                ((ti_hbm, raw_ti), (si_hbm, raw_si), (tt_hbm, raw_tt), (st_hbm, raw_st))
+                ((ti_hbm, raw_ti), (tt_hbm, raw_tt), (si_hbm, raw_si), (st_hbm, raw_st))
             )
-        ])
+        ]
+        for k, (r, m) in enumerate((CHUNKS[0], (CHUNKS[1][0], ROWS - CHUNKS[1][0])))
+    ]
     for group in loads:
         for copy in group:
             copy.start()
     barrier = pltpu.get_barrier_semaphore()
-    for dev in (across, sibling, before):
-        pl.semaphore_signal(barrier, inc=1, device_id=dev, device_id_type=MESH)
     relays = place % HOP == 1
 
+    def report(dev, to):
+        pl.semaphore_signal(barrier, inc=1, device_id=(dev[0], dev[1] // 2 * 2 + to), device_id_type=MESH)
+
+    report(across, 0)
+    report(before, 1)
+
+    @pl.when(core == 1)
+    def _():
+        report(sibling, 0)
+
     @pl.when(place == 1 + HOP)
     def _():
-        pl.semaphore_signal(barrier, inc=1, device_id=at(HOP, False), device_id_type=MESH)
+        report(at(HOP, False), 1)
 
     @pl.when(place == 1)
     def _():
-        pl.semaphore_signal(barrier, inc=1, device_id=at(HOP - RUN, True), device_id_type=MESH)
+        report(at(HOP - RUN, True), 1)
 
     @pl.when(place == 0)
     def _():
-        pl.semaphore_signal(barrier, inc=1, device_id=at(1, False), device_id_type=MESH)
-
+        report(at(1, False), 1)
+
+    def wait_gate(counter, amount):
+        @pl.when(core == counter)
+        def _():
+            pl.semaphore_wait(barrier, amount)
+            pl.semaphore_signal(gate, inc=1, device_id=sibling, device_id_type=MESH)
+
+        @pl.when(core != counter)
+        def _():
+            pl.semaphore_wait(gate, 1)
 
     def unit(raw, rows, out, at, keep=None):
         wide = raw[rows].astype(jnp.float32)
@@ -116,20 +133,20 @@
         own = pl.ds(r, m)
         po, ps = prev_at(k)
         y_cp.append((
-            remote(TI.at[own], TI.at[pl.ds(ROWS + r, m)], y_s.at[2 * k], y_r.at[2 * k], across),
-            remote(SI.at[own], SI.at[pl.ds(ROWS + r, m)], y_s.at[2 * k + 1], y_r.at[2 * k + 1], across),
+            remote(TI.at[own], TI.at[pl.ds(ROWS + r, m)], y_s.at[0], y_r.at[2 * k], across),
+            remote(SI.at[own], SI.at[pl.ds(ROWS + r, m)], y_s.at[1], y_r.at[2 * k + 1], across),
         ))
         z_cp.append((
-            remote(TT.at[own], TT.at[po], z_s.at[2 * k], z_r.at[2 * k], after),
-            remote(ST.at[own], ST.at[po], z_s.at[2 * k + 1], z_r.at[2 * k + 1], after),
+            remote(TT.at[own], TT.at[po], z_s.at[2 * (k in FAR)], z_r.at[2 * k], after),
+            remote(ST.at[own], ST.at[po], z_s.at[2 * (k in FAR) + 1], z_r.at[2 * k + 1], after),
         ))
         d_cp.append((
-            remote(TT.at[own], TT.at[pl.ds(ROWS + r, m)], d_s.at[2 * k], d_r.at[2 * k], sibling),
-            remote(ST.at[own], ST.at[pl.ds(ROWS + r, m)], d_s.at[2 * k + 1], d_r.at[2 * k + 1], sibling),
+            remote(TT.at[own], TT.at[pl.ds(ROWS + r, m)], d_s.at[0], d_r.at[0], sibling),
+            remote(ST.at[own], ST.at[pl.ds(ROWS + r, m)], d_s.at[1], d_r.at[1], sibling),
         ))
         f_cp.append((
-            remote(TT.at[po], TT.at[ps], f_s.at[2 * k], f_r.at[2 * k], sibling),
-            remote(ST.at[po], ST.at[ps], f_s.at[2 * k + 1], f_r.at[2 * k + 1], sibling),
+            remote(TT.at[po], TT.at[ps], f_s.at[0], f_r.at[2 * k], sibling),
+            remote(ST.at[po], ST.at[ps], f_s.at[1], f_r.at[2 * k + 1], sibling),
         ))
         if k in FAR:
             down, over, home = at(-HOP, False), at(RUN - HOP, True), at(-1, False)
@@ -138,9 +155,9 @@
             for half, (text, stay) in enumerate(((TT, far_t), (ST, far_s))):
                 n = 2 * (k - FAR[0]) + half
                 pairs.append((
-                    remote(text.at[own], stay.at[stop], q_s.at[n], q_r.at[n], down),
-                    remote(stay.at[stop], stay.at[stop], q_s.at[n], q_r.at[n], over),
-                    remote(stay.at[stop], text.at[po], q_s.at[n], z_r.at[2 * k + half], home),
+                    remote(text.at[own], stay.at[stop], q_s.at[half], q_r.at[n], down),
+                    remote(stay.at[stop], stay.at[stop], q_s.at[half], q_r.at[n], over),
+                    remote(stay.at[stop], text.at[po], q_s.at[half], z_r.at[2 * k + half], home),
                 ))
             far_cp.extend(pairs)
 
@@ -167,19 +184,19 @@
         copy.wait()
     own = pl.ds(*CHUNKS[0])
     unit(raw_ti, own, TI, own)
+    unit(raw_si, own, SI, own, inv_i)
+    wait_gate(0, 3)
+    for half in (0, 1):
+        y_cp[0][half].start()
     unit(raw_tt, own, TT, own)
-    pl.semaphore_wait(barrier, jnp.where(relays, 4, 3))
-    y_cp[0][0].start()
-    z_cp[0][0].start()
-    unit(raw_si, own, SI, own, inv_i)
     unit(raw_st, own, ST, own, inv_t)
-    y_cp[0][1].start()
-    z_cp[0][1].start()
-    d_cp[0][0].start()
-    d_cp[0][1].start()
-    for group in loads[1:]:
-        for copy in group:
-            copy.wait()
+    for half in (0, 1):
+        d_cp[0][half].start()
+    for copy in loads[1]:
+        copy.wait()
+    wait_gate(1, jnp.where(relays, 4, 2))
+    for half in (0, 1):
+        z_cp[0][half].start()
     for k in FAR:
         own = pl.ds(*CHUNKS[k])
         for half, norm in ((0, (raw_tt, own, TT, own)), (1, (raw_st, own, ST, own, inv_t))):
@@ -216,9 +233,9 @@
 
     teach(0, ROWS, 0, ROWS)
     study(0, ROWS, 0, ROWS)
-    for k in range(N_CH):
-        for copy in d_cp[k]:
-            copy.wait_recv()
+    for half, text in enumerate((TT, ST)):
+        theirs = text.at[pl.ds(ROWS, ROWS)]
+        remote(theirs, theirs, d_s.at[half], d_r.at[half], sibling).wait_recv()
     teach(0, ROWS, ROWS, ROWS)
     study(0, ROWS, ROWS, ROWS)
 
@@ -242,15 +259,15 @@
                 pass_on(hop, first, last)
 
     yp_cp = [
-        remote(y_out.at[pl.ds(c * PULL, PULL)], y_in.at[pl.ds(c * PULL, PULL)], yp_s.at[c], yp_r.at[c], across)
+        remote(y_out.at[pl.ds(c * PULL, PULL)], y_in.at[pl.ds(c * PULL, PULL)], yp_s.at[0], yp_r.at[c], across)
         for c in range(N_PULL)
     ]
     zp_cp = [
-        remote(z_out.at[pl.ds(r, m)], z_in.at[pl.ds(r, m)], zp_s.at[k], zp_r.at[k], before)
+        remote(z_out.at[pl.ds(r, m)], z_in.at[pl.ds(r, m)], zp_s.at[0], zp_r.at[k], before)
         for k, (r, m) in enumerate(CHUNKS)
     ]
     dp_cp = [
-        remote(dp_out.at[pl.ds(r, m)], dp_in.at[pl.ds(r, m)], dp_s.at[k], dp_r.at[k], sibling)
+        remote(dp_out.at[pl.ds(r, m)], dp_in.at[pl.ds(r, m)], dp_s.at[0], dp_r.at[k], sibling)
         for k, (r, m) in enumerate(CHUNKS)
     ]
     dt_cp = remote(dt_out, dt_in, dt_s.at[0], dt_r.at[0], sibling)
@@ -394,19 +411,27 @@
         if text is not None:
             finish_text(text)
 
-    for n, copies in enumerate(far_cp):
-        @pl.when(relays)
-        def _():
-            copies[0].wait_send()
-
-        @pl.when(place != RUN - 1)
-        def _():
-            z_cp[FAR[n // 2]][n % 2].wait_send()
-
-    near = [z_cp[k] for k in range(N_CH) if k not in FAR]
-    for group in (*y_cp, *near, *d_cp, *f_cp, yp_cp, zp_cp, dp_cp, (dt_cp,)):
-        for copy in group:
-            copy.wait_send()
+    near = CHUNKS[FAR[0]][0]
+    sent = [
+        (y_out, yp_s.at[0]), (z_out, zp_s.at[0]), (dp_out, dp_s.at[0]), (dt_out, dt_s.at[0]),
+    ]
+    for half, (image, text) in enumerate(((TI, TT), (SI, ST))):
+        whole = pl.ds(0, ROWS)
+        sent += [(image.at[whole], y_s.at[half]), (text.at[whole], d_s.at[half]), (text.at[whole], f_s.at[half])]
+        sent += [(text.at[pl.ds(0, near)], z_s.at[half])]
+    for src, sem in sent:
+        remote(src, src, sem, sem, sibling).wait_send()
+
+    @pl.when(relays)
+    def _():
+        for half, stay in enumerate((far_t, far_s)):
+            remote(stay, stay, q_s.at[half], q_s.at[half], sibling).wait_send()
+
+    @pl.when(place != RUN - 1)
+    def _():
+        for half, text in enumerate((TT, ST)):
+            rows = text.at[pl.ds(near, ROWS - near)]
+            remote(rows, rows, z_s.at[2 + half], z_s.at[2 + half], sibling).wait_send()
 
 
 def write_kernel(gi_ref, gt_ref, gi_hbm, gt_hbm, sem):
@@ -442,11 +467,10 @@
             part(full), part(full), part(full),
             *[part(half)] * 8,
             pltpu.VMEM((FAR_ROWS, D_T), half), pltpu.VMEM((FAR_ROWS, D_S), half),
-            dma((N_CH, 4)),
-            dma((2 * len(FAR),)), dma((2 * len(FAR),)),
-            *[dma((2 * N_CH,))] * 8,
-            dma((N_PULL,)), dma((N_PULL,)), dma((1,)), dma((1,)),
-            *[dma((N_CH,))] * 4,
+            pltpu.SemaphoreType.REGULAR, dma((2, 4)),
+            dma((2,)), dma((2 * len(FAR),)),
+            dma((2,)), dma((2 * N_CH,)), dma((4,)), dma((2 * N_CH,)), dma((2,)), dma((2,)), dma((2,)), dma((2 * N_CH,)),
+            dma((1,)), dma((N_PULL,)), dma((1,)), dma((1,)), dma((1,)), dma((N_CH,)), dma((1,)), dma((N_CH,)),
         ],
         compiler_params=pltpu.CompilerParams(
             collective_id=0, has_side_effects=True, vmem_limit_bytes=44 * 2**20,

time: 63.3 us -> 62.6 us (0.989)
  Pallas kernels: 59.7 us -> 59 us
    pallas_call x1, Pallas kernels: 58.3 us -> 57.6 us  [per_device(): pl.pallas_call(kernel, out_shape=(jax.ShapeDtypeStruct((ROWS, D_S), full)...]
where the time goes in v5:
time: 62.6 us; the launch traced here: 62.4 us
  Pallas kernels  59 us (94%)
  between operations  3.4 us (5%)
    pallas_call x1, Pallas kernels, per_device(): pl.pallas_call(kernel, out_shape=(jax.ShapeDtypeStruct((ROWS, D_S), full)...  57.6 us
    pallas_call x1, Pallas kernels, per_device(): pl.pallas_call(write_kernel, out_shape=(jax.ShapeDtypeStruct((ROWS, D_S),...  1.43 us

profile of v5, /device:TPU:1, one launch (start us, length us, event | category | flops | bytes accessed | tf_op | source)
XLA Modules:
  0.0 62.4 jit_solution(7859337544781232475)
XLA Ops:
  3.2 57.6 %shard_map.95 = (f32[384,768]{1,0:T(8,128)S(1)}, f32[384,768]{1,0:T(8,128)S(1)}) custom-call(f32[1]{0:T(128)S(6)} %copy.10.ss_ref, f32[1]{0:T(128)S(6)} %copy.11.sb_ref, f32[1]{0:T(128)S(6)} %copy.12.ts_ref, f32[1]{0:T(128)S(6)} %copy.13.tb_ref, bf16[384,768]{1,0:T(8,128)(2,1)} %si_hbm.1, bf16[384,768]{1,0:T(8,128)(2,1)} %st_hbm.1, ...), custom_call_target="tpu_custom_call" | custom-call | tf_op jit(solution)/shard_map/pallas_call | solution.py:456
  60.8 1.4 %shard_map.96 = (f32[384,768]{1,0:T(8,128)}, f32[384,768]{1,0:T(8,128)}) custom-call(f32[384,768]{1,0:T(8,128)S(1)} %get-tuple-element.4.gi_ref, f32[384,768]{1,0:T(8,128)S(1)} %get-tuple-element.5.gt_ref), custom_call_target="tpu_custom_call" | custom-call | tf_op jit(solution)/shard_map/pallas_call | solution.py:479

commit v6 on v5

--- a/solution.py
+++ b/solution.py
@@ -335,12 +335,18 @@
         gt_ref[early] = first_text(0, ROWS + r)
         early_across(j)
         step(last)
-        study(ROWS + r, m, OWN_TEXT, j - OWN_TEXT)
+        second = OWN_TEXT + 2 * CHUNKS[1][0]
+        study(ROWS + r, m, OWN_TEXT, second - OWN_TEXT)
         prev_leave(gt_ref[early] + first_text(ROWS + r, m), 0, 1)
+        study(ROWS + r, m, second, j - second)
+        prev_pull(1, 2)
+        f_cp[last][1].wait_recv()
+        study(ROWS, FIRST, j, 2 * m)
+        late_across(j)
+        prev_send(0)
         study(ROWS + r, m, 0, OWN_TEXT)
-        f_cp[last][1].wait_recv()
-        study(0, 2 * ROWS, j, 2 * m)
-        late_across(j)
+        study(0, ROWS, j, 2 * m)
+        study(ROWS + FIRST, ROWS - FIRST, j, 2 * m)
 
     @pl.when(place == 0)
     def _():
@@ -363,6 +369,7 @@
                 f_cp[k][half].wait_recv()
             tile(0, ROWS + r, OWN_TEXT, j - OWN_TEXT)
         early_across(j)
+        width = 2 * (ROWS - mid)
         for half, tile in ((0, teach), (1, study)):
             for k in (*range(SPLIT, FAR[0]), last):
                 arrive(k, half)
@@ -370,13 +377,17 @@
             tile(ROWS + r, m, 0, j)
             if half == 1:
                 prev_pull(0, 1)
+                prev_pull(1, 2)
             for k in range(SPLIT, N_CH):
                 f_cp[k][half].wait_recv()
-            tile(0, 2 * ROWS, j, 2 * (ROWS - mid))
+            if half == 0:
+                tile(0, 2 * ROWS, j, width)
+        study(ROWS, FIRST, j, width)
         late_across(j)
-
-    prev_send(0)
-    prev_pull(1, 2)
+        prev_send(0)
+        study(0, ROWS, j, width)
+        study(ROWS + FIRST, ROWS - FIRST, j, width)
+
     across_pull(2, 4)
     prev_send(1)
     prev_pull(2, N_CH)

time: 62.6 us -> 61.7 us (0.986)
  Pallas kernels: 59 us -> 58.2 us
    pallas_call x1, Pallas kernels: 57.6 us -> 56.7 us  [per_device(): pl.pallas_call(kernel, out_shape=(jax.ShapeDtypeStruct((ROWS, D_S), full)...]
where the time goes in v6:
time: 61.7 us; the launch traced here: 61.6 us
  Pallas kernels  58.2 us (94%)
  between operations  3.4 us (6%)
    pallas_call x1, Pallas kernels, per_device(): pl.pallas_call(kernel, out_shape=(jax.ShapeDtypeStruct((ROWS, D_S), full)...  56.7 us
    pallas_call x1, Pallas kernels, per_device(): pl.pallas_call(write_kernel, out_shape=(jax.ShapeDtypeStruct((ROWS, D_S),...  1.43 us

profile of v6, /device:TPU:1, one launch (start us, length us, event | category | flops | bytes accessed | tf_op | source)
XLA Modules:
  0.0 61.6 jit_solution(9511775696487215316)
XLA Ops:
  3.2 56.7 %shard_map.95 = (f32[384,768]{1,0:T(8,128)S(1)}, f32[384,768]{1,0:T(8,128)S(1)}) custom-call(f32[1]{0:T(128)S(6)} %copy.10.ss_ref, f32[1]{0:T(128)S(6)} %copy.11.sb_ref, f32[1]{0:T(128)S(6)} %copy.12.ts_ref, f32[1]{0:T(128)S(6)} %copy.13.tb_ref, bf16[384,768]{1,0:T(8,128)(2,1)} %si_hbm.1, bf16[384,768]{1,0:T(8,128)(2,1)} %st_hbm.1, ...), custom_call_target="tpu_custom_call" | custom-call | tf_op jit(solution)/shard_map/pallas_call | solution.py:467
  59.9 1.4 %shard_map.96 = (f32[384,768]{1,0:T(8,128)}, f32[384,768]{1,0:T(8,128)}) custom-call(f32[384,768]{1,0:T(8,128)S(1)} %get-tuple-element.4.gi_ref, f32[384,768]{1,0:T(8,128)S(1)} %get-tuple-element.5.gt_ref), custom_call_target="tpu_custom_call" | custom-call | tf_op jit(solution)/shard_map/pallas_call | solution.py:490

commit v7 on v6

--- a/solution.py
+++ b/solution.py
@@ -23,7 +23,7 @@
 N_WRITE = 2
 PULL = 64
 FIRST = 2 * PULL
-N_PULL = ROWS // PULL
+PIECES = ((0, FIRST), *((r, PULL) for r in range(FIRST, ROWS, PULL)))
 OWN_TEXT = 2 * ROWS
 
 NT = (((1,), (1,)), ((), ()))
@@ -259,8 +259,8 @@
                 pass_on(hop, first, last)
 
     yp_cp = [
-        remote(y_out.at[pl.ds(c * PULL, PULL)], y_in.at[pl.ds(c * PULL, PULL)], yp_s.at[0], yp_r.at[c], across)
-        for c in range(N_PULL)
+        remote(y_out.at[pl.ds(r, m)], y_in.at[pl.ds(r, m)], yp_s.at[0], yp_r.at[c], across)
+        for c, (r, m) in enumerate(PIECES)
     ]
     zp_cp = [
         remote(z_out.at[pl.ds(r, m)], z_in.at[pl.ds(r, m)], zp_s.at[0], zp_r.at[k], before)
@@ -268,7 +268,7 @@
     ]
     dp_cp = [
         remote(dp_out.at[pl.ds(r, m)], dp_in.at[pl.ds(r, m)], dp_s.at[0], dp_r.at[k], sibling)
-        for k, (r, m) in enumerate(CHUNKS)
+        for k, (r, m) in enumerate((*CHUNKS[:2], (CHUNKS[2][0], ROWS - CHUNKS[2][0])))
     ]
     dt_cp = remote(dt_out, dt_in, dt_s.at[0], dt_r.at[0], sibling)
 
@@ -278,10 +278,11 @@
     def text_pull(j, n):
         return lax.dot_general(W[:, pl.ds(j, n)], SI[...], TN, preferred_element_type=jnp.float32)
 
-    def across_pull(c, n):
-        y_out[pl.ds(c * PULL, n * PULL)] = image_pull(ROWS + c * PULL, n * PULL).astype(jnp.bfloat16)
-        for i in range(c, c + n):
-            yp_cp[i].start()
+    def across_rest():
+        rest = ROWS - FIRST
+        y_out[pl.ds(FIRST, rest)] = image_pull(ROWS + FIRST, rest).astype(jnp.bfloat16)
+        for copy in yp_cp[1:]:
+            copy.start()
 
     def early_across(j):
         gi_ref[pl.ds(0, FIRST)] = jnp.dot(
@@ -294,8 +295,7 @@
             preferred_element_type=jnp.float32,
         )
         y_out[pl.ds(0, FIRST)] = (gi_ref[pl.ds(0, FIRST)] + rest).astype(jnp.bfloat16)
-        for i in range(FIRST // PULL):
-            yp_cp[i].start()
+        yp_cp[0].start()
 
     def first_text(i, m):
         m0 = CHUNKS[0][1]
@@ -310,7 +310,7 @@
             mine = 2 * (at - r)
             prev_own[pl.ds(at, m)] = pull[mine:mine + m]
             dp_out[pl.ds(at, m)] = pull[mine + m:mine + 2 * m].astype(jnp.bfloat16)
-            dp_cp[k].start()
+        dp_cp[first].start()
 
     def prev_pull(first, last):
         r, rows = CHUNKS[first][0], sum(m for _, m in CHUNKS[first:last])
@@ -319,7 +319,8 @@
     def prev_send(k):
         r, m = CHUNKS[k]
         rows = pl.ds(r, m)
-        dp_cp[k].wait_recv()
+        if k < len(dp_cp):
+            dp_cp[k].wait_recv()
         z_out[rows] = (prev_own[rows] + dp_in[rows].astype(jnp.float32)).astype(jnp.bfloat16)
         zp_cp[k].start()
 
@@ -388,7 +389,7 @@
         study(0, ROWS, j, width)
         study(ROWS + FIRST, ROWS - FIRST, j, width)
 
-    across_pull(2, 4)
+    across_rest()
     prev_send(1)
     prev_pull(2, N_CH)
     for k in range(2, N_CH):
@@ -405,7 +406,7 @@
         return (grown - row * jnp.sum(row * grown, axis=-1, keepdims=True)) * inverse
 
     def finish_image(c):
-        rows = pl.ds(c * PULL, PULL)
+        rows = pl.ds(*PIECES[c])
         yp_cp[c].wait_recv()
         pull = img_own[rows] + y_in[rows].astype(jnp.float32)
         gi_ref[rows] = project(pull, raw_si[rows], inv_i[rows], s_scale)
@@ -417,8 +418,9 @@
         pull = txt_own[rows] + dt_in[rows].astype(jnp.float32) + z_in[rows].astype(jnp.float32)
         gt_ref[rows] = project(pull, raw_st[rows], inv_t[rows], s_scale)
 
-    for image, text in ((0, 0), (1, None), (2, 1), (3, 2), (4, 3), (5, 4)):
-        finish_image(image)
+    for image, text in ((None, 0), (0, None), (1, 1), (2, None), (3, 2), (None, 3), (4, 4)):
+        if image is not None:
+            finish_image(image)
         if text is not None:
             finish_text(text)
 
@@ -481,7 +483,7 @@
             pltpu.SemaphoreType.REGULAR, dma((2, 4)),
             dma((2,)), dma((2 * len(FAR),)),
             dma((2,)), dma((2 * N_CH,)), dma((4,)), dma((2 * N_CH,)), dma((2,)), dma((2,)), dma((2,)), dma((2 * N_CH,)),
-            dma((1,)), dma((N_PULL,)), dma((1,)), dma((1,)), dma((1,)), dma((N_CH,)), dma((1,)), dma((N_CH,)),
+            dma((1,)), dma((len(PIECES),)), dma((1,)), dma((1,)), dma((1,)), dma((3,)), dma((1,)), dma((N_CH,)),
         ],
         compiler_params=pltpu.CompilerParams(
             collective_id=0, has_side_effects=True, vmem_limit_bytes=44 * 2**20,

time: 61.7 us -> 61.7 us (level)
  no operation moved by 1% of the time
where the time goes in v7:
time: 61.7 us; the launch traced here: 61.5 us
  Pallas kernels  58.1 us (94%)
  between operations  3.4 us (6%)
    pallas_call x1, Pallas kernels, per_device(): pl.pallas_call(kernel, out_shape=(jax.ShapeDtypeStruct((ROWS, D_S), full)...  56.7 us
    pallas_call x1, Pallas kernels, per_device(): pl.pallas_call(write_kernel, out_shape=(jax.ShapeDtypeStruct((ROWS, D_S),...  1.43 us

profile of v7, /device:TPU:1, one launch (start us, length us, event | category | flops | bytes accessed | tf_op | source)
XLA Modules:
  0.0 61.5 jit_solution(7875249919532293306)
XLA Ops:
  3.2 56.7 %shard_map.95 = (f32[384,768]{1,0:T(8,128)S(1)}, f32[384,768]{1,0:T(8,128)S(1)}) custom-call(f32[1]{0:T(128)S(6)} %copy.10.ss_ref, f32[1]{0:T(128)S(6)} %copy.11.sb_ref, f32[1]{0:T(128)S(6)} %copy.12.ts_ref, f32[1]{0:T(128)S(6)} %copy.13.tb_ref, bf16[384,768]{1,0:T(8,128)(2,1)} %si_hbm.1, bf16[384,768]{1,0:T(8,128)(2,1)} %st_hbm.1, ...), custom_call_target="tpu_custom_call" | custom-call | tf_op jit(solution)/shard_map/pallas_call | solution.py:469
  59.9 1.4 %shard_map.96 = (f32[384,768]{1,0:T(8,128)}, f32[384,768]{1,0:T(8,128)}) custom-call(f32[384,768]{1,0:T(8,128)S(1)} %get-tuple-element.4.gi_ref, f32[384,768]{1,0:T(8,128)S(1)} %get-tuple-element.5.gt_ref), custom_call_target="tpu_custom_call" | custom-call | tf_op jit(solution)/shard_map/pallas_call | solution.py:492
